TPU v7x, 512 devices: a whole 4x4x16 slice. The times are simulated.
512 devices in a mesh: term: 32 (over z_hi, y, core), sec: 16 (over x, z_lo).
Axes of the slice: x: 4, y: 4, z: 16 (z_hi: 4, z_lo: 4; z = z_hi * 4 + z_lo), core: 2. Of those that a mesh axis runs over, the one named last changes fastest.
Arguments:
- wavefunction: bfloat16 [16, 512, 512], P('sec', 'term'), may hold values from -6 to 6
- left_operator_blocks: bfloat16 [128, 16, 512, 512], P('term', 'sec'), may hold values from -0.5 to 0.5
- right_ops: bfloat16 [128, 16, 512, 512], P('term', 'sec'), may hold values from -0.046875 to 0.046875
- charge_shift: int32 [128], replicated, may hold values from -2 to 2, as said below
- assignment: int32 [128], P('term'), may hold values from 0 to 127, each once
- sector_size: int32 [16], replicated, may hold values from 128 to 512, as said below
Outputs:
- sigma: bfloat16 [16, 512, 512], P('sec', 'term')
Inputs may be any that keep to these rules, and one draw needn't show every extreme that they name: `sector_size`: some sector has exactly 512 live rows. `assignment`: each term appears in exactly one slot. `charge_shift`: every offset from -2 to 2 is taken by at least 25 terms.
All inputs are finite; a program needn't handle non-finite values.
Results may differ from a plain program's by a relative error of at most 0.0049.
Values may be sent and summed in bfloat16 or wider, within the bound.
No kernel may reach another device: no remote copies, remote signals or barrier semaphores. Data moves between devices by JAX's collectives and lax.ppermute only.
A program may use at most 64 MiB of HBM per device.

v0:
```python
import jax
import jax.numpy as jnp
from jax import lax
from jax.sharding import PartitionSpec as P


def from_behind(block, axis, distance):
    devices = range(lax.axis_size(axis))
    route = [(i - distance, i) for i in devices if i - distance in devices]
    return lax.ppermute(block, axis, route)


def nearby_whole(whole):
    pieces = []
    for offset in (-2, -1, 0, 1, 2):
        if offset == 0:
            pieces.append(whole)
        else:
            pieces.append(from_behind(whole, "sec", -offset))
    return jnp.concatenate(pieces, axis=0)


def body(wavefunction, left_operator_blocks, right_ops, charge_shift, assignment, sector_size):
    slab_rows = wavefunction.shape[1]
    nblk = wavefunction.shape[2]
    own_sector = lax.axis_index("sec")
    sector_ids = jnp.arange(sector_size.shape[0], dtype=jnp.int32)
    own_size = jnp.sum(jnp.where(sector_ids == own_sector, sector_size, 0))
    row_start = lax.axis_index("term") * slab_rows
    row_ids = row_start + jnp.arange(slab_rows, dtype=jnp.int32)
    column_index_list = jnp.arange(nblk, dtype=jnp.int32)
    sector_band_mask = (row_ids[:, None] < own_size) & (column_index_list[None, :] < own_size)
    slab = jnp.where(sector_band_mask[None], wavefunction, jnp.zeros_like(wavefunction))
    whole = lax.all_gather(slab, "term", axis=1, tiled=True)
    blocks = nearby_whole(whole)
    term_ids = jnp.arange(charge_shift.shape[0], dtype=jnp.int32)
    shifts = jnp.sum(
        jnp.where(term_ids[None, :] == assignment[:, None], charge_shift[None, :], 0), axis=1
    )
    slot_count = left_operator_blocks.shape[0]
    total = jnp.zeros((lax.axis_size("term") * slab_rows, nblk), jnp.float32)
    for term_position in range(slot_count):
        source = lax.dynamic_index_in_dim(blocks, shifts[term_position] + 2, 0, keepdims=False)
        left_rows = left_operator_blocks[term_position, 0]
        inner = jnp.dot(left_rows, source, preferred_element_type=jnp.float32).astype(jnp.bfloat16)
        total = total + lax.dot_general(
            inner,
            right_ops[term_position, 0],
            (((1,), (1,)), ((), ())),
            preferred_element_type=jnp.float32,
        )
    summed = lax.psum_scatter(total, "term", scatter_dimension=0, tiled=True)
    result = jnp.where(sector_band_mask, summed, 0.0).astype(jnp.bfloat16)
    return result[None]


def solution(mesh):
    placed = (
        P("sec", "term", None),
        P("term", "sec", None, None),
        P("term", "sec", None, None),
        P(),
        P("term"),
        P(),
    )
    return jax.shard_map(
        body, mesh=mesh, in_specs=placed, out_specs=P("sec", "term", None), check_vma=False
    )
```

profile of v0, /device:TPU:6, one launch (start us, length us, event | category | flops | bytes accessed | tf_op | source)
XLA Modules:
  0.0 271.8 jit_solution(181079870596791616)
XLA Ops:
  6.5 0.0 reduce-scatter.2.cloned.1.call-start
  6.5 1.3 fusion.50
  7.8 0.6 iota_compare_fusion.1
  8.5 0.7 add_compare_fusion
  9.1 0.8 and_select_fusion
  9.9 60.7 %all_gather.3 = bf16[1,512,512]{2,1,0:T(8,128)(2,1)S(1)} all-gather(bf16[1,16,512]{2,1,0:T(8,128)(2,1)S(1)} %and_select_fusion), channel_id=1, replica_groups=mesh['term'=32,'sec'=16] {'term'}, dimensions={1}, use_global_device_ids=true | all-gather | bytes 540672 | tf_op jit(solution)/shard_map/all_gather | solution.py:34
  70.7 3.4 %collective-permute-start = (bf16[1,512,512]{2,1,0:T(8,128)(2,1)S(1)}, bf16[1,512,512]{2,1,0:T(8,128)(2,1)}, u32[]{:S(2)}, u32[]{:S(2)}) collective-permute-start(bf16[1,512,512]{2,1,0:T(8,128)(2,1)S(1)} %all_gather.3), channel_id=1, source_target_pairs={{0,2},{1,3},{2,4},{3,5},{4,6},{5,7},{6,8},{7,9},{8,10},{9,11},{10,... | collective-permute-start | bytes 1572872 | tf_op jit(solution)/shard_map/ppermute | solution.py:10
  74.1 2.9 %collective-permute-start.1 = (bf16[1,512,512]{2,1,0:T(8,128)(2,1)S(1)}, bf16[1,512,512]{2,1,0:T(8,128)(2,1)}, u32[]{:S(2)}, u32[]{:S(2)}) collective-permute-start(bf16[1,512,512]{2,1,0:T(8,128)(2,1)S(1)} %all_gather.3), channel_id=1, source_target_pairs={{0,1},{1,2},{2,3},{3,4},{4,5},{5,6},{6,7},{7,8},{8,9},{9,10},{10,1... | collective-permute-start | bytes 1572872 | tf_op jit(solution)/shard_map/ppermute | solution.py:10
  77.1 5.6 %collective-permute-start.2 = (bf16[1,512,512]{2,1,0:T(8,128)(2,1)S(1)}, bf16[1,512,512]{2,1,0:T(8,128)(2,1)}, u32[]{:S(2)}, u32[]{:S(2)}) collective-permute-start(bf16[1,512,512]{2,1,0:T(8,128)(2,1)S(1)} %all_gather.3), channel_id=1, source_target_pairs={{1,0},{2,1},{3,2},{4,3},{5,4},{6,5},{7,6},{8,7},{9,8},{10,9},{11,1... | collective-permute-start | bytes 1572872 | tf_op jit(solution)/shard_map/ppermute | solution.py:10
  82.7 1.9 collective-permute-start.3
  84.6 0.9 select_reduce_fusion
  85.4 0.6 fusion.51
  90.8 21.4 %collective-permute-done = bf16[1,512,512]{2,1,0:T(8,128)(2,1)} collective-permute-done((bf16[1,512,512]{2,1,0:T(8,128)(2,1)S(1)}, bf16[1,512,512]{2,1,0:T(8,128)(2,1)}, u32[]{:S(2)}, u32[]{:S(2)}) %collective-permute-start) | collective-permute-done | bytes 524320 | tf_op jit(solution)/shard_map/ppermute | solution.py:10
  112.2 1.1 constant_dynamic-update-slice_fusion.4
  113.3 0.0 collective-permute-done.1
  113.3 1.1 constant_dynamic-update-slice_fusion.3
  114.4 0.0 collective-permute-done.2
  114.4 1.1 constant_dynamic-update-slice_fusion.1
  115.5 4.1 %collective-permute-done.3 = bf16[1,512,512]{2,1,0:T(8,128)(2,1)} collective-permute-done((bf16[1,512,512]{2,1,0:T(8,128)(2,1)S(1)}, bf16[1,512,512]{2,1,0:T(8,128)(2,1)}, u32[]{:S(2)}, u32[]{:S(2)}) %collective-permute-start.3) | collective-permute-done | bytes 524320 | tf_op jit(solution)/shard_map/ppermute | solution.py:10
  119.6 1.1 constant_dynamic-update-slice_fusion
  120.6 0.0 copy-start
  120.7 1.5 copy-done
  122.2 3.1 %fusion = f32[512,512]{1,0:T(8,128)} fusion(bf16[4,1,512,512]{3,2,1,0:T(8,128)(2,1)} %param.8, bf16[4,1,512,512]{3,2,1,0:T(8,128)(2,1)} %param.7, bf16[5,512,512]{2,1,0:T(8,128)(2,1)S(1)} %constant_dynamic-update-slice_fusion, s32[]{:T(128)S(6)} %select_n.32), kind=kOutput, calls=%fused_computation.7 | convolution fusion | flops 537133056 | bytes 2621444 | tf_op jit(solution)/shard_map/dot_general | solution.py:46
  125.2 2.6 convolution_add_fusion.2
  127.8 2.2 convolution_add_fusion.1
  130.0 3.2 %convolution_add_fusion = f32[512,512]{1,0:T(8,128)} fusion(f32[512,512]{1,0:T(8,128)S(1)} %convolution_add_fusion.1, bf16[4,1,512,512]{3,2,1,0:T(8,128)(2,1)} %param.8, bf16[4,1,512,512]{3,2,1,0:T(8,128)(2,1)} %param.7, bf16[5,512,512]{2,1,0:T(8,128)(2,1)} %copy-done, s32[]{:T(128)S(6)} %select_n.35), kind=kOutput, calls=%fused_computation | convolution fusion | flops 537395200 | bytes 3670020 | tf_op jit(solution)/shard_map/dot_general | solution.py:46
  133.3 0.0 reduce-scatter.2.cloned.1.call-update
  133.3 130.2 %reduce-scatter.2.cloned.1.call-done = f32[16,512]{1,0:T(8,128)} async-done(((f32[512,512]{1,0:T(8,128)}), f32[16,512]{1,0:T(8,128)}) %reduce-scatter.2.cloned.1.call-update) | async-done | bytes 32784 | tf_op jit(solution)/shard_map/reduce_scatter | solution.py:52
  263.5 1.4 fusion.41
  (1 shorter events, 0.0 us)
Async XLA Ops:
  6.5 257.0 %reduce-scatter.2.cloned.1.call-start = ((), (), s32[]{:S(2)}) async-start(), calls=%async_computation.1 | async-start | bytes 1081344 | tf_op jit(solution)/shard_map/reduce_scatter | solution.py:52
  70.7 41.5 %collective-permute-start = (bf16[1,512,512]{2,1,0:T(8,128)(2,1)S(1)}, bf16[1,512,512]{2,1,0:T(8,128)(2,1)}, u32[]{:S(2)}, u32[]{:S(2)}) collective-permute-start(bf16[1,512,512]{2,1,0:T(8,128)(2,1)S(1)} %all_gather.3), channel_id=1, source_target_pairs={{0,2},{1,3},{2,4},{3,5},{4,6},{5,7},{6,8},{7,9},{8,10},{9,11},{10,... | collective-permute-start | bytes 1572872 | tf_op jit(solution)/shard_map/ppermute | solution.py:10
  74.1 39.2 %collective-permute-start.1 = (bf16[1,512,512]{2,1,0:T(8,128)(2,1)S(1)}, bf16[1,512,512]{2,1,0:T(8,128)(2,1)}, u32[]{:S(2)}, u32[]{:S(2)}) collective-permute-start(bf16[1,512,512]{2,1,0:T(8,128)(2,1)S(1)} %all_gather.3), channel_id=1, source_target_pairs={{0,1},{1,2},{2,3},{3,4},{4,5},{5,6},{6,7},{7,8},{8,9},{9,10},{10,1... | collective-permute-start | bytes 1572872 | tf_op jit(solution)/shard_map/ppermute | solution.py:10
  77.1 37.3 %collective-permute-start.2 = (bf16[1,512,512]{2,1,0:T(8,128)(2,1)S(1)}, bf16[1,512,512]{2,1,0:T(8,128)(2,1)}, u32[]{:S(2)}, u32[]{:S(2)}) collective-permute-start(bf16[1,512,512]{2,1,0:T(8,128)(2,1)S(1)} %all_gather.3), channel_id=1, source_target_pairs={{1,0},{2,1},{3,2},{4,3},{5,4},{6,5},{7,6},{8,7},{9,8},{10,9},{11,1... | collective-permute-start | bytes 1572872 | tf_op jit(solution)/shard_map/ppermute | solution.py:10
  82.7 36.9 %collective-permute-start.3 = (bf16[1,512,512]{2,1,0:T(8,128)(2,1)S(1)}, bf16[1,512,512]{2,1,0:T(8,128)(2,1)}, u32[]{:S(2)}, u32[]{:S(2)}) collective-permute-start(bf16[1,512,512]{2,1,0:T(8,128)(2,1)S(1)} %all_gather.3), channel_id=1, source_target_pairs={{2,0},{3,1},{4,2},{5,3},{6,4},{7,5},{8,6},{9,7},{10,8},{11,9},{12,... | collective-permute-start | bytes 1572872 | tf_op jit(solution)/shard_map/ppermute | solution.py:10
  120.6 1.5 copy-start
Sparse Core Ops, SparseCore 0:
  133.4 130.0 reduce-scatter.1
where the time goes:
time: 273 us; the launch traced here: 272 us
  waiting for transfers between devices  156 us (57%)
  blocking collectives  60.7 us (22%)
  between operations  18.3 us (7%)
  starting transfers between devices  13.9 us (5%)
  matrix products  11.1 us (4%)
  local copies, waits for them, and re-layouts  6.45 us (2%)
  other arithmetic  5.68 us (2%)
    reduce_scatter x1, waiting for transfers between devices, body(): summed = lax.psum_scatter(total, 'term', scatter_dimension=0, tiled=True)  130 us
    all_gather x1, blocking collectives, body(): whole = lax.all_gather(slab, 'term', axis=1, tiled=True)  60.7 us
    ppermute x4, waiting for transfers between devices, from_behind(): return lax.ppermute(block, axis, route)  25.5 us
    ppermute x4, starting transfers between devices, from_behind(): return lax.ppermute(block, axis, route)  13.9 us
    dot_general x4, matrix products, body(): lax.dot_general(inner, right_ops[term_position, 0], (((1,), (1,)), ((), (...  11.1 us
  transfers between devices with their start and end apart: 5, of which 3 were waited for; matrix products, arithmetic and copies ran while one was open for 2% of the time, Pallas kernels for 0%

commit v1 on v0

v1 whole, which is shorter than its diff:
```python
import functools

import jax
import jax.numpy as jnp
from jax import lax
from jax.experimental import pallas as pl
from jax.experimental.pallas import tpu as pltpu
from jax.sharding import Mesh
from jax.sharding import PartitionSpec as P

ZH, Y, CORE, X, ZL = 4, 4, 2, 4, 4
SECTORS = X * ZL
NEAR = 5
SLAB = 16
F32, BF16 = jnp.float32, jnp.bfloat16

SMEM = pl.BlockSpec(memory_space=pltpu.SMEM)
VMEM = pl.BlockSpec(memory_space=pltpu.VMEM)
MIB = 1 << 20


def own_sector():
    return lax.axis_index("x") * ZL + lax.axis_index("zl")


def live_mask(size, nblk):
    term = (lax.axis_index("zh") * Y + lax.axis_index("y")) * CORE + lax.axis_index("core")
    rows = term * SLAB + lax.broadcasted_iota(jnp.int32, (SLAB, nblk), 0)
    cols = lax.broadcasted_iota(jnp.int32, (SLAB, nblk), 1)
    return (rows < size) & (cols < size)


def spread_kernel(size_ref, slab_ref, out_ref):
    slab = slab_ref[0]
    mask = live_mask(size_ref[own_sector()], slab.shape[1])
    live = jnp.where(mask, slab.astype(F32), 0.0).astype(BF16)
    for copy in range(out_ref.shape[0]):
        out_ref[copy] = live


def pick_kernel(column_ref, beside_ref, out_ref):
    zl = lax.axis_index("zl")
    for place in range(NEAR):
        sector = zl + place - 2

        @pl.when((sector >= 0) & (sector < ZL))
        def _():
            block = column_ref[jnp.clip(sector, 0, ZL - 1)]
            for y in range(Y):
                out_ref[y, place] = block

        @pl.when((sector < 0) | (sector >= ZL))
        def _():
            block = beside_ref[jnp.clip(jnp.where(sector < 0, sector + 2, sector - ZL), 0, 1)]
            for y in range(Y):
                out_ref[y, place] = block


def product_kernel(shift_ref, assign_ref, mine_ref, other_ref, left_ref, right_ref, keep_ref, send_ref, blocks, total):
    core = lax.axis_index("core")
    nblk = left_ref.shape[-1]
    for y in range(Y):
        for place in range(NEAR):
            blocks[place, :, y, pl.ds(core, 1)] = mine_ref[y, place][:, None]
            blocks[place, :, y, pl.ds(1 - core, 1)] = other_ref[y, place][:, None]
    slots = left_ref.shape[0]
    for slot in range(slots):
        place = shift_ref[assign_ref[slot]] + 2
        source = blocks[place].reshape(nblk, nblk)
        inner = jnp.dot(left_ref[slot, 0], source, preferred_element_type=F32).astype(BF16)
        part = lax.dot_general(inner, right_ref[slot, 0], (((1,), (1,)), ((), ())), preferred_element_type=F32)
        part = part.reshape(total.shape)
        if slot == 0:
            total[...] = part
        else:
            total[...] += part
    keep_ref[...] = total[:, core]
    send_ref[...] = total[:, 1 - core].astype(BF16)


def join_kernel(keep_ref, got_ref, out_ref):
    out_ref[...] = (keep_ref[...] + got_ref[...].astype(F32)).astype(BF16)


def finish_kernel(size_ref, parts_ref, out_ref):
    nblk = parts_ref.shape[-1]
    total = jnp.sum(parts_ref[...].astype(F32), axis=0)
    mask = live_mask(size_ref[own_sector()], nblk)
    out_ref[0] = jnp.where(mask, total, 0.0).astype(BF16)


def call(kernel, out_shape, in_specs, scratch=(), flops=0, moved=MIB, limit=16 * MIB):
    many = isinstance(out_shape, (tuple, list))
    return pl.pallas_call(
        kernel,
        out_shape=out_shape,
        in_specs=in_specs,
        out_specs=tuple(VMEM for _ in out_shape) if many else VMEM,
        scratch_shapes=scratch,
        cost_estimate=pl.CostEstimate(flops=flops, bytes_accessed=moved, transcendentals=0),
        compiler_params=pltpu.CompilerParams(vmem_limit_bytes=limit),
    )


def shape(*dims, dtype=BF16):
    return jax.ShapeDtypeStruct(dims, dtype)


def next_x(block):
    route = []
    for x in range(X):
        for zl in range(ZL):
            to = x + 1 if zl < ZL // 2 else x - 1
            if 0 <= to < X:
                route.append((x * ZL + zl, to * ZL + zl))
    return lax.ppermute(block, ("x", "zl"), route)


def swap_core(block):
    return lax.ppermute(block, "core", [(0, 1), (1, 0)])


def body(wavefunction, left_operator_blocks, right_ops, charge_shift, assignment, sector_size):
    nblk = wavefunction.shape[2]
    slots = left_operator_blocks.shape[0]
    spread = call(spread_kernel, shape(ZL * ZH, SLAB, nblk), [SMEM, VMEM])(sector_size, wavefunction)
    column = lax.all_to_all(spread, ("zl", "zh"), 0, 0, tiled=True).reshape(ZL, ZH, SLAB, nblk)
    low = lax.axis_index("zl") < ZL // 2
    beside = next_x(jnp.where(low, column[2:], column[:2]))
    near = call(pick_kernel, shape(Y, NEAR, ZH, SLAB, nblk), [VMEM, VMEM])(column, beside)
    mine = lax.all_to_all(near, "y", 0, 0, tiled=True)
    other = swap_core(mine)
    keep, send = call(
        product_kernel,
        (shape(ZH * Y, SLAB, nblk, dtype=F32), shape(ZH * Y, SLAB, nblk)),
        [SMEM, SMEM, VMEM, VMEM, VMEM, VMEM],
        scratch=[
            pltpu.VMEM((NEAR, ZH, Y, CORE, SLAB, nblk), BF16),
            pltpu.VMEM((ZH * Y, CORE, SLAB, nblk), F32),
        ],
        flops=slots * 4 * nblk**3,
        moved=8 * MIB,
        limit=32 * MIB,
    )(charge_shift, assignment, mine, other, left_operator_blocks, right_ops)
    joined = call(join_kernel, shape(ZH * Y, SLAB, nblk), [VMEM, VMEM])(keep, swap_core(send))
    parts = lax.all_to_all(joined, ("zh", "y"), 0, 0, tiled=True)
    return call(finish_kernel, shape(1, SLAB, nblk), [SMEM, VMEM])(sector_size, parts)


def solution(mesh):
    grid = Mesh(mesh.devices.reshape(ZH, Y, CORE, X, ZL), ("zh", "y", "core", "x", "zl"))
    term, sec = ("zh", "y", "core"), ("x", "zl")
    placed = (
        P(sec, term, None),
        P(term, sec, None, None),
        P(term, sec, None, None),
        P(),
        P(term),
        P(),
    )
    return jax.shard_map(body, mesh=grid, in_specs=placed, out_specs=P(sec, term, None), check_vma=False)
```

time: 273 us -> 104 us (0.38)
  waiting for transfers between devices: 156 us -> 27.4 us
  between operations: 18.3 us -> 0.11 us
  blocking collectives: 60.7 us -> 47 us
  matrix products: 11.1 us -> 0 us
  starting transfers between devices: 13.9 us -> 20.5 us
  Pallas kernels: 0 us -> 5.8 us
  other arithmetic: 5.68 us -> 0.02 us
  local copies, waits for them, and re-layouts: 6.45 us -> 1.4 us
    reduce_scatter x1 -> x0, waiting for transfers between devices: 130 us -> none  [body(): summed = lax.psum_scatter(total, 'term', scatter_dimension=0, tiled=True)]
    all_gather x1 -> x0, blocking collectives: 60.7 us -> none  [body(): whole = lax.all_gather(slab, 'term', axis=1, tiled=True)]
    all_to_all x0 -> x2, blocking collectives: none -> 47 us  [the longest x1 28.1 us: body(): parts = lax.all_to_all(joined, ('zh', 'y'), 0, 0, tiled=True)]
    all_to_all x0 -> x1, waiting for transfers between devices: none -> 17.5 us  [body(): lax.all_to_all(spread, ('zl', 'zh'), 0, 0, tiled=True)]
    ppermute x4 -> x3, waiting for transfers between devices: 25.5 us -> 9.91 us  [the longest x1 5.56 us: next_x(): return lax.ppermute(block, ('x', 'zl'), route)]
    all_to_all x0 -> x1, starting transfers between devices: none -> 15.2 us  [body(): lax.all_to_all(spread, ('zl', 'zh'), 0, 0, tiled=True)]
    dot_general x4 -> x0, matrix products: 11.1 us -> none  [body(): lax.dot_general(inner, right_ops[term_position, 0], (((1,), (1,)), ((), (...]
    ppermute x4 -> x3, starting transfers between devices: 13.9 us -> 5.28 us  [the longest x2 3.98 us: swap_core(): return lax.ppermute(block, 'core', [(0, 1), (1, 0)])]
  transfers between devices with their start and end apart: 5 -> 4, of which waited for: 3 -> 4; matrix products, arithmetic and copies ran while one was open for 2% -> 0% of each run, Pallas kernels for 0% -> 0%
where the time goes in v1:
time: 104 us; the launch traced here: 102 us
  blocking collectives  47 us (45%)
  waiting for transfers between devices  27.4 us (26%)
  starting transfers between devices  20.5 us (20%)
  Pallas kernels  5.8 us (6%)
  local copies, waits for them, and re-layouts  1.4 us (1%)
    all_to_all x1, blocking collectives, body(): parts = lax.all_to_all(joined, ('zh', 'y'), 0, 0, tiled=True)  28.1 us
    all_to_all x1, blocking collectives, body(): mine = lax.all_to_all(near, 'y', 0, 0, tiled=True)  18.8 us
    all_to_all x1, waiting for transfers between devices, body(): lax.all_to_all(spread, ('zl', 'zh'), 0, 0, tiled=True)  17.5 us
    all_to_all x1, starting transfers between devices, body(): lax.all_to_all(spread, ('zl', 'zh'), 0, 0, tiled=True)  15.2 us
    ppermute x1, waiting for transfers between devices, next_x(): return lax.ppermute(block, ('x', 'zl'), route)  5.56 us
    ppermute x2, waiting for transfers between devices, swap_core(): return lax.ppermute(block, 'core', [(0, 1), (1, 0)])  4.35 us
    ppermute x2, starting transfers between devices, swap_core(): return lax.ppermute(block, 'core', [(0, 1), (1, 0)])  3.98 us
    pallas_call x1, Pallas kernels, body(): call(product_kernel, (shape(ZH * Y, SLAB, nblk, dtype=F32), shape(ZH * Y,...  3.12 us
  transfers between devices with their start and end apart: 4, of which 4 were waited for; matrix products, arithmetic and copies ran while one was open for 0% of the time, Pallas kernels for 0%

profile of v1, /device:TPU:6, one launch (start us, length us, event | category | flops | bytes accessed | tf_op | source)
XLA Modules:
  0.0 102.2 jit_solution(15164684523380749459)
XLA Ops:
  0.0 0.0 copy-start
  0.0 0.7 copy-done
  0.7 0.0 copy-start.1
  0.7 0.7 copy-done.1
  1.4 1.3 %shard_map.64 = bf16[16,16,512]{2,1,0:T(8,128)(2,1)} custom-call(s32[16]{0:T(128)S(1)} %copy-done.1, bf16[1,16,512]{2,1,0:T(8,128)(2,1)S(1)} %copy-done), custom_call_target="tpu_custom_call" | custom-call | bytes 1048576 | tf_op jit(solution)/shard_map/pallas_call | solution.py:126
  2.7 15.2 %all-to-all-start = ((bf16[16,16,512]{2,1,0:T(8,128)(2,1)}), bf16[16,16,512]{2,1,0:T(8,128)(2,1)S(1)}, u32[]{:S(2)}, u32[]{:S(2)}) async-start(bf16[16,16,512]{2,1,0:T(8,128)(2,1)} %shard_map.64), calls=%async_computation | async-start | bytes 524288 | tf_op jit(solution)/shard_map/all_to_all | solution.py:127
  17.9 17.5 %all-to-all-done = bf16[16,16,512]{2,1,0:T(8,128)(2,1)S(1)} async-done(((bf16[16,16,512]{2,1,0:T(8,128)(2,1)}), bf16[16,16,512]{2,1,0:T(8,128)(2,1)S(1)}, u32[]{:S(2)}, u32[]{:S(2)}) %all-to-all-start) | async-done | bytes 262176 | tf_op jit(solution)/shard_map/all_to_all | solution.py:127
  35.4 1.3 %collective-permute-start = (bf16[2,4,16,512]{3,2,1,0:T(8,128)(2,1)S(1)}, bf16[2,4,16,512]{3,2,1,0:T(8,128)(2,1)S(1)}, u32[]{:S(2)}, u32[]{:S(2)}) collective-permute-start(bf16[2,4,16,512]{3,2,1,0:T(8,128)(2,1)S(1)} %bitcast.3), channel_id=1, source_target_pairs={{0,4},{1,5},{4,8},{5,9},{6,2},{7,3},{8,12},{9,13},{10,6},{11,7},{1... | collective-permute-start | bytes 393224 | tf_op jit(solution)/shard_map/ppermute | solution.py:116
  36.7 5.6 %collective-permute-done.beside_ref = bf16[2,4,16,512]{3,2,1,0:T(8,128)(2,1)S(1)} collective-permute-done((bf16[2,4,16,512]{3,2,1,0:T(8,128)(2,1)S(1)}, bf16[2,4,16,512]{3,2,1,0:T(8,128)(2,1)S(1)}, u32[]{:S(2)}, u32[]{:S(2)}) %collective-permute-start) | collective-permute-done | bytes 131104 | tf_op jit(solution)/shard_map/ppermute | solution.py:116
  42.2 0.0 copy-start.4
  42.2 0.1 shard_map.65
  42.4 0.0 copy-start.3
  42.4 0.0 copy-start.5
  42.4 0.0 copy-start.6
  42.4 18.8 %all_to_all.15.mine_ref = bf16[4,5,4,16,512]{4,3,2,1,0:T(8,128)(2,1)S(1)} all-to-all(bf16[4,5,4,16,512]{4,3,2,1,0:T(8,128)(2,1)S(1)} %shard_map.65), channel_id=1, replica_groups=mesh['zh'=4,'y'=4,'core'=2,'x'=4,'zl'=4] {'y'}, dimensions={0} | all-to-all | bytes 2621440 | tf_op jit(solution)/shard_map/all_to_all | solution.py:131
  61.3 1.9 %collective-permute-start.1 = (bf16[4,5,4,16,512]{4,3,2,1,0:T(8,128)(2,1)S(1)}, bf16[4,5,4,16,512]{4,3,2,1,0:T(8,128)(2,1)S(1)}, u32[]{:S(2)}, u32[]{:S(2)}) collective-permute-start(bf16[4,5,4,16,512]{4,3,2,1,0:T(8,128)(2,1)S(1)} %all_to_all.15.mine_ref), channel_id=1, source_target_pairs={{0,16},{16,0},{1,17},{17,1},{2,18},{18,2},{3,19},{19,3},{4,20},{20... | collective-permute-start | bytes 3932168 | tf_op jit(solution)/shard_map/ppermute | solution.py:120
  63.2 3.0 %collective-permute-done.1.other_ref = bf16[4,5,4,16,512]{4,3,2,1,0:T(8,128)(2,1)S(1)} collective-permute-done((bf16[4,5,4,16,512]{4,3,2,1,0:T(8,128)(2,1)S(1)}, bf16[4,5,4,16,512]{4,3,2,1,0:T(8,128)(2,1)S(1)}, u32[]{:S(2)}, u32[]{:S(2)}) %collective-permute-start.1) | collective-permute-done | bytes 1310752 | tf_op jit(solution)/shard_map/ppermute | solution.py:120
  66.2 0.0 copy-done.4
  66.2 0.0 copy-done.3
  66.2 0.0 copy-done.5
  66.2 0.0 copy-done.6
  66.2 3.1 %shard_map.66 = (f32[16,16,512]{2,1,0:T(8,128)S(1)}, bf16[16,16,512]{2,1,0:T(8,128)(2,1)S(1)}) custom-call(s32[128]{0:T(128)S(1)} %copy-done.5, s32[4]{0:T(128)S(1)} %copy-done.6, bf16[4,5,4,16,512]{4,3,2,1,0:T(8,128)(2,1)S(1)} %all_to_all.15.mine_ref, bf16[4,5,4,16,512]{4,3,2,1,0:T(8,128)(2,1)S(1)} %collective-permute-done.1.other_ref, ...), custom_call_target="tpu_custom_call" | custom-call | flops 2147483648 | bytes 8388608 | tf_op jit(solution)/shard_map/pallas_call | solution.py:133
  69.3 0.0 copy-start.2
  69.3 2.1 %collective-permute-start.2 = (bf16[16,16,512]{2,1,0:T(8,128)(2,1)S(1)}, bf16[16,16,512]{2,1,0:T(8,128)(2,1)S(1)}, u32[]{:S(2)}, u32[]{:S(2)}) collective-permute-start(bf16[16,16,512]{2,1,0:T(8,128)(2,1)S(1)} %get-tuple-element.8), channel_id=1, source_target_pairs={{0,16},{16,0},{1,17},{17,1},{2,18},{18,2},{3,19},{19,3},{4,20},{20... | collective-permute-start | bytes 786440 | tf_op jit(solution)/shard_map/ppermute | solution.py:120
  71.4 1.3 %collective-permute-done.2.got_ref = bf16[16,16,512]{2,1,0:T(8,128)(2,1)S(1)} collective-permute-done((bf16[16,16,512]{2,1,0:T(8,128)(2,1)S(1)}, bf16[16,16,512]{2,1,0:T(8,128)(2,1)S(1)}, u32[]{:S(2)}, u32[]{:S(2)}) %collective-permute-start.2) | collective-permute-done | bytes 262176 | tf_op jit(solution)/shard_map/ppermute | solution.py:120
  72.8 0.1 shard_map.67
  72.8 28.1 %all_to_all.16.parts_ref = bf16[16,16,512]{2,1,0:T(8,128)(2,1)S(1)} all-to-all(bf16[16,16,512]{2,1,0:T(8,128)(2,1)S(1)} %shard_map.67), channel_id=1, replica_groups=mesh['zh'=4,'y'=4,'core'=2,'x'=4,'zl'=4] {'zh','y'}, dimensions={0} | all-to-all | bytes 524288 | tf_op jit(solution)/shard_map/all_to_all | solution.py:146
  101.0 0.0 copy-done.2
  101.0 1.2 %shard_map.68 = bf16[1,16,512]{2,1,0:T(8,128)(2,1)} custom-call(s32[16]{0:T(128)S(1)} %copy-done.2, bf16[16,16,512]{2,1,0:T(8,128)(2,1)S(1)} %all_to_all.16.parts_ref), custom_call_target="tpu_custom_call" | custom-call | bytes 1048576 | tf_op jit(solution)/shard_map/pallas_call | solution.py:147
  (1 shorter events, 0.0 us)
Async XLA Ops:
  0.0 0.7 copy-start
  0.7 0.7 copy-start.1
  2.7 32.7 %all-to-all-start = ((bf16[16,16,512]{2,1,0:T(8,128)(2,1)}), bf16[16,16,512]{2,1,0:T(8,128)(2,1)S(1)}, u32[]{:S(2)}, u32[]{:S(2)}) async-start(bf16[16,16,512]{2,1,0:T(8,128)(2,1)} %shard_map.64), calls=%async_computation | async-start | bytes 524288 | tf_op jit(solution)/shard_map/all_to_all | solution.py:127
  35.4 6.9 %collective-permute-start = (bf16[2,4,16,512]{3,2,1,0:T(8,128)(2,1)S(1)}, bf16[2,4,16,512]{3,2,1,0:T(8,128)(2,1)S(1)}, u32[]{:S(2)}, u32[]{:S(2)}) collective-permute-start(bf16[2,4,16,512]{3,2,1,0:T(8,128)(2,1)S(1)} %bitcast.3), channel_id=1, source_target_pairs={{0,4},{1,5},{4,8},{5,9},{6,2},{7,3},{8,12},{9,13},{10,6},{11,7},{1... | collective-permute-start | bytes 393224 | tf_op jit(solution)/shard_map/ppermute | solution.py:116
  42.2 23.9 %copy-start.4 = (bf16[4,1,512,512]{3,2,1,0:T(8,128)(2,1)S(1)}, bf16[4,1,512,512]{3,2,1,0:T(8,128)(2,1)}, u32[]{:S(2)}) copy-start(bf16[4,1,512,512]{3,2,1,0:T(8,128)(2,1)} %right_ref.1) | copy-start | bytes 6291460
  42.4 23.8 %copy-start.3 = (bf16[4,1,512,512]{3,2,1,0:T(8,128)(2,1)S(1)}, bf16[4,1,512,512]{3,2,1,0:T(8,128)(2,1)}, u32[]{:S(2)}) copy-start(bf16[4,1,512,512]{3,2,1,0:T(8,128)(2,1)} %left_ref.1) | copy-start | bytes 6291460
  42.4 23.8 %copy-start.5 = (s32[128]{0:T(128)S(1)}, s32[128]{0:T(128)}, u32[]{:S(2)}) copy-start(s32[128]{0:T(128)} %shift_ref.1) | copy-start | bytes 1540
  42.4 23.8 %copy-start.6 = (s32[4]{0:T(128)S(1)}, s32[4]{0:T(128)}, u32[]{:S(2)}) copy-start(s32[4]{0:T(128)} %assign_ref.1) | copy-start | bytes 52
  61.3 4.9 %collective-permute-start.1 = (bf16[4,5,4,16,512]{4,3,2,1,0:T(8,128)(2,1)S(1)}, bf16[4,5,4,16,512]{4,3,2,1,0:T(8,128)(2,1)S(1)}, u32[]{:S(2)}, u32[]{:S(2)}) collective-permute-start(bf16[4,5,4,16,512]{4,3,2,1,0:T(8,128)(2,1)S(1)} %all_to_all.15.mine_ref), channel_id=1, source_target_pairs={{0,16},{16,0},{1,17},{17,1},{2,18},{18,2},{3,19},{19,3},{4,20},{20... | collective-permute-start | bytes 3932168 | tf_op jit(solution)/shard_map/ppermute | solution.py:120
  69.3 31.6 %copy-start.2 = (s32[16]{0:T(128)S(1)}, s32[16]{0:T(128)}, u32[]{:S(2)}) copy-start(s32[16]{0:T(128)} %size_ref.3) | copy-start | bytes 196
  69.3 3.4 %collective-permute-start.2 = (bf16[16,16,512]{2,1,0:T(8,128)(2,1)S(1)}, bf16[16,16,512]{2,1,0:T(8,128)(2,1)S(1)}, u32[]{:S(2)}, u32[]{:S(2)}) collective-permute-start(bf16[16,16,512]{2,1,0:T(8,128)(2,1)S(1)} %get-tuple-element.8), channel_id=1, source_target_pairs={{0,16},{16,0},{1,17},{17,1},{2,18},{18,2},{3,19},{19,3},{4,20},{20... | collective-permute-start | bytes 786440 | tf_op jit(solution)/shard_map/ppermute | solution.py:120

commit v2 on v1

--- a/solution.py
+++ b/solution.py
@@ -30,12 +30,9 @@
     return (rows < size) & (cols < size)
 
 
-def spread_kernel(size_ref, slab_ref, out_ref):
-    slab = slab_ref[0]
-    mask = live_mask(size_ref[own_sector()], slab.shape[1])
-    live = jnp.where(mask, slab.astype(F32), 0.0).astype(BF16)
-    for copy in range(out_ref.shape[0]):
-        out_ref[copy] = live
+def outgoing_kernel(column_ref, out_ref):
+    low = lax.axis_index("zl") < ZL // 2
+    out_ref[...] = column_ref[pl.ds(jnp.where(low, 2, 0), 2)]
 
 
 def pick_kernel(column_ref, beside_ref, out_ref):
@@ -56,13 +53,19 @@
                 out_ref[y, place] = block
 
 
-def product_kernel(shift_ref, assign_ref, mine_ref, other_ref, left_ref, right_ref, keep_ref, send_ref, blocks, total):
+def product_kernel(size_ref, shift_ref, assign_ref, mine_ref, other_ref, left_ref, right_ref, keep_ref, send_ref, blocks, total):
     core = lax.axis_index("core")
     nblk = left_ref.shape[-1]
+    dims = (ZH, SLAB, nblk)
+    inside = lax.broadcasted_iota(jnp.int32, dims, 0) * (Y * CORE * SLAB) + lax.broadcasted_iota(jnp.int32, dims, 1)
+    cols = lax.broadcasted_iota(jnp.int32, dims, 2)
+    sizes = [size_ref[jnp.clip(own_sector() + place - 2, 0, SECTORS - 1)] for place in range(NEAR)]
     for y in range(Y):
-        for place in range(NEAR):
-            blocks[place, :, y, pl.ds(core, 1)] = mine_ref[y, place][:, None]
-            blocks[place, :, y, pl.ds(1 - core, 1)] = other_ref[y, place][:, None]
+        for ref, of in ((mine_ref, core), (other_ref, 1 - core)):
+            reach = jnp.maximum(inside + (y * CORE + of) * SLAB, cols)
+            for place in range(NEAR):
+                live = jnp.where(reach < sizes[place], ref[y, place].astype(F32), 0.0)
+                blocks[place, :, y, pl.ds(of, 1)] = live.astype(BF16)[:, None]
     slots = left_ref.shape[0]
     for slot in range(slots):
         place = shift_ref[assign_ref[slot]] + 2
@@ -78,8 +81,9 @@
     send_ref[...] = total[:, 1 - core].astype(BF16)
 
 
-def join_kernel(keep_ref, got_ref, out_ref):
-    out_ref[...] = (keep_ref[...] + got_ref[...].astype(F32)).astype(BF16)
+def join_kernel(keep_ref, both_ref, out_ref):
+    got = both_ref[1 - lax.axis_index("core")]
+    out_ref[...] = (keep_ref[...] + got.astype(F32)).astype(BF16)
 
 
 def finish_kernel(size_ref, parts_ref, out_ref):
@@ -89,7 +93,7 @@
     out_ref[0] = jnp.where(mask, total, 0.0).astype(BF16)
 
 
-def call(kernel, out_shape, in_specs, scratch=(), flops=0, moved=MIB, limit=16 * MIB):
+def call(kernel, out_shape, in_specs, scratch=(), flops=0, moved=MIB, limit=4 * MIB):
     many = isinstance(out_shape, (tuple, list))
     return pl.pallas_call(
         kernel,
@@ -123,26 +127,25 @@
 def body(wavefunction, left_operator_blocks, right_ops, charge_shift, assignment, sector_size):
     nblk = wavefunction.shape[2]
     slots = left_operator_blocks.shape[0]
-    spread = call(spread_kernel, shape(ZL * ZH, SLAB, nblk), [SMEM, VMEM])(sector_size, wavefunction)
+    spread = jnp.broadcast_to(wavefunction, (ZL * ZH, SLAB, nblk))
     column = lax.all_to_all(spread, ("zl", "zh"), 0, 0, tiled=True).reshape(ZL, ZH, SLAB, nblk)
-    low = lax.axis_index("zl") < ZL // 2
-    beside = next_x(jnp.where(low, column[2:], column[:2]))
+    beside = next_x(call(outgoing_kernel, shape(2, ZH, SLAB, nblk), [VMEM])(column))
     near = call(pick_kernel, shape(Y, NEAR, ZH, SLAB, nblk), [VMEM, VMEM])(column, beside)
     mine = lax.all_to_all(near, "y", 0, 0, tiled=True)
     other = swap_core(mine)
     keep, send = call(
         product_kernel,
         (shape(ZH * Y, SLAB, nblk, dtype=F32), shape(ZH * Y, SLAB, nblk)),
-        [SMEM, SMEM, VMEM, VMEM, VMEM, VMEM],
+        [SMEM, SMEM, SMEM, VMEM, VMEM, VMEM, VMEM],
         scratch=[
             pltpu.VMEM((NEAR, ZH, Y, CORE, SLAB, nblk), BF16),
             pltpu.VMEM((ZH * Y, CORE, SLAB, nblk), F32),
         ],
         flops=slots * 4 * nblk**3,
         moved=8 * MIB,
-        limit=32 * MIB,
-    )(charge_shift, assignment, mine, other, left_operator_blocks, right_ops)
-    joined = call(join_kernel, shape(ZH * Y, SLAB, nblk), [VMEM, VMEM])(keep, swap_core(send))
+        limit=12 * MIB,
+    )(sector_size, charge_shift, assignment, mine, other, left_operator_blocks, right_ops)
+    joined = call(join_kernel, shape(ZH * Y, SLAB, nblk), [VMEM, VMEM])(keep, lax.all_gather(send, "core"))
     parts = lax.all_to_all(joined, ("zh", "y"), 0, 0, tiled=True)
     return call(finish_kernel, shape(1, SLAB, nblk), [SMEM, VMEM])(sector_size, parts)
 

time: 104 us -> 101 us (0.971)
  blocking collectives: 47 us -> 81.7 us
  waiting for transfers between devices: 27.4 us -> 8.56 us
  starting transfers between devices: 20.5 us -> 3.2 us
    all_to_all x0 -> x1, blocking collectives: none -> 32.5 us  [body(): lax.all_to_all(spread, ('zl', 'zh'), 0, 0, tiled=True)]
    all_to_all x1 -> x0, waiting for transfers between devices: 17.5 us -> none  [body(): lax.all_to_all(spread, ('zl', 'zh'), 0, 0, tiled=True)]
    all_to_all x1 -> x0, starting transfers between devices: 15.2 us -> none  [body(): lax.all_to_all(spread, ('zl', 'zh'), 0, 0, tiled=True)]
    all_gather x0 -> x1, blocking collectives: none -> 2.18 us  [body(): lax.all_gather(send, 'core')]
    ppermute x2 -> x1, starting transfers between devices: 3.98 us -> 1.91 us  [swap_core(): return lax.ppermute(block, 'core', [(0, 1), (1, 0)])]
    unnamed x14 -> x10, local copies, waits for them, and re-layouts: 1.4 us -> 0.03 us
    ppermute x2 -> x1, waiting for transfers between devices: 4.35 us -> 3 us  [swap_core(): return lax.ppermute(block, 'core', [(0, 1), (1, 0)])]
    pallas_call x1, Pallas kernels: 1.29 us -> 0.01 us  [body(): call(outgoing_kernel, shape(2, ZH, SLAB, nblk), [VMEM])(column)]
  transfers between devices with their start and end apart: 4 -> 2, of which waited for: 4 -> 2; matrix products, arithmetic and copies ran while one was open for 0% -> 0% of each run, Pallas kernels for 0% -> 0%
where the time goes in v2:
time: 101 us; the launch traced here: 99.4 us
  blocking collectives  81.7 us (81%)
  waiting for transfers between devices  8.56 us (8%)
  Pallas kernels  5.11 us (5%)
  starting transfers between devices  3.2 us (3%)
    all_to_all x1, blocking collectives, body(): lax.all_to_all(spread, ('zl', 'zh'), 0, 0, tiled=True)  32.5 us
    all_to_all x1, blocking collectives, body(): parts = lax.all_to_all(joined, ('zh', 'y'), 0, 0, tiled=True)  28.1 us
    all_to_all x1, blocking collectives, body(): mine = lax.all_to_all(near, 'y', 0, 0, tiled=True)  18.8 us
    ppermute x1, waiting for transfers between devices, next_x(): return lax.ppermute(block, ('x', 'zl'), route)  5.56 us
    pallas_call x1, Pallas kernels, body(): call(product_kernel, (shape(ZH * Y, SLAB, nblk, dtype=F32), shape(ZH * Y,...  3.73 us
    ppermute x1, waiting for transfers between devices, swap_core(): return lax.ppermute(block, 'core', [(0, 1), (1, 0)])  3 us
    all_gather x1, blocking collectives, body(): lax.all_gather(send, 'core')  2.18 us
  transfers between devices with their start and end apart: 2, of which 2 were waited for; matrix products, arithmetic and copies ran while one was open for 0% of the time, Pallas kernels for 0%

profile of v2, /device:TPU:6, one launch (start us, length us, event | category | flops | bytes accessed | tf_op | source)
XLA Modules:
  0.0 99.4 jit_solution(17596639799272724122)
XLA Ops:
  0.0 0.7 broadcast_in_dim.8
  0.7 32.5 %all_to_all.15 = bf16[16,16,512]{2,1,0:T(8,128)(2,1)S(1)} all-to-all(bf16[16,16,512]{2,1,0:T(8,128)(2,1)S(1)} %broadcast_in_dim.8), channel_id=1, replica_groups=mesh['zh'=4,'y'=4,'core'=2,'x'=4,'zl'=4] {'zl','zh'}, dimensions={0} | all-to-all | bytes 524288 | tf_op jit(solution)/shard_map/all_to_all | solution.py:131
  33.2 1.3 %collective-permute-start = (bf16[2,4,16,512]{3,2,1,0:T(8,128)(2,1)S(1)}, bf16[2,4,16,512]{3,2,1,0:T(8,128)(2,1)S(1)}, u32[]{:S(2)}, u32[]{:S(2)}) collective-permute-start(bf16[2,4,16,512]{3,2,1,0:T(8,128)(2,1)S(1)} %shard_map.64), channel_id=1, source_target_pairs={{0,4},{1,5},{4,8},{5,9},{6,2},{7,3},{8,12},{9,13},{10,6},{11,7},{1... | collective-permute-start | bytes 393224 | tf_op jit(solution)/shard_map/ppermute | solution.py:120
  34.5 5.6 %collective-permute-done.beside_ref = bf16[2,4,16,512]{3,2,1,0:T(8,128)(2,1)S(1)} collective-permute-done((bf16[2,4,16,512]{3,2,1,0:T(8,128)(2,1)S(1)}, bf16[2,4,16,512]{3,2,1,0:T(8,128)(2,1)S(1)}, u32[]{:S(2)}, u32[]{:S(2)}) %collective-permute-start) | collective-permute-done | bytes 131104 | tf_op jit(solution)/shard_map/ppermute | solution.py:120
  40.1 0.0 copy-start.2
  40.1 0.1 shard_map.65
  40.2 0.0 copy-start
  40.3 0.0 copy-start.1
  40.3 0.0 copy-start.3
  40.3 0.0 copy-start.4
  40.3 18.8 %all_to_all.16.mine_ref = bf16[4,5,4,16,512]{4,3,2,1,0:T(8,128)(2,1)S(1)} all-to-all(bf16[4,5,4,16,512]{4,3,2,1,0:T(8,128)(2,1)S(1)} %shard_map.65), channel_id=1, replica_groups=mesh['zh'=4,'y'=4,'core'=2,'x'=4,'zl'=4] {'y'}, dimensions={0} | all-to-all | bytes 2621440 | tf_op jit(solution)/shard_map/all_to_all | solution.py:134
  59.1 1.9 %collective-permute-start.1 = (bf16[4,5,4,16,512]{4,3,2,1,0:T(8,128)(2,1)S(1)}, bf16[4,5,4,16,512]{4,3,2,1,0:T(8,128)(2,1)S(1)}, u32[]{:S(2)}, u32[]{:S(2)}) collective-permute-start(bf16[4,5,4,16,512]{4,3,2,1,0:T(8,128)(2,1)S(1)} %all_to_all.16.mine_ref), channel_id=1, source_target_pairs={{0,16},{16,0},{1,17},{17,1},{2,18},{18,2},{3,19},{19,3},{4,20},{20... | collective-permute-start | bytes 3932168 | tf_op jit(solution)/shard_map/ppermute | solution.py:124
  61.1 3.0 %collective-permute-done.1.other_ref = bf16[4,5,4,16,512]{4,3,2,1,0:T(8,128)(2,1)S(1)} collective-permute-done((bf16[4,5,4,16,512]{4,3,2,1,0:T(8,128)(2,1)S(1)}, bf16[4,5,4,16,512]{4,3,2,1,0:T(8,128)(2,1)S(1)}, u32[]{:S(2)}, u32[]{:S(2)}) %collective-permute-start.1) | collective-permute-done | bytes 1310752 | tf_op jit(solution)/shard_map/ppermute | solution.py:124
  64.1 0.0 copy-done.2
  64.1 0.0 copy-done
  64.1 0.0 copy-done.1
  64.1 0.0 copy-done.3
  64.1 0.0 copy-done.4
  64.1 3.7 %shard_map.66 = (f32[16,16,512]{2,1,0:T(8,128)S(1)}, bf16[16,16,512]{2,1,0:T(8,128)(2,1)S(1)}) custom-call(s32[16]{0:T(128)S(1)} %copy-done, s32[128]{0:T(128)S(1)} %copy-done.3, s32[4]{0:T(128)S(1)} %copy-done.4, bf16[4,5,4,16,512]{4,3,2,1,0:T(8,128)(2,1)S(1)} %all_to_all.16.mine_ref, bf16[4,5,4,16,512]{4,3,2,1,0:T(8,128)(2,1)S(1)} %collective-permute-done.1.other_ref, ...), custom_call_target="tpu_custom_call" | custom-call | flops 2147483648 | bytes 8388608 | tf_op jit(solution)/shard_map/pallas_call | solution.py:136
  67.8 2.2 %all-gather = bf16[32,16,512]{2,1,0:T(8,128)(2,1)S(1)} all-gather(bf16[16,16,512]{2,1,0:T(8,128)(2,1)S(1)} %get-tuple-element.8), channel_id=2, replica_groups=mesh['zh'=4,'y'=4,'core'=2,'x'=4,'zl'=4] {'core'}, dimensions={0}, use_global_device_ids=true | all-gather | bytes 786432 | tf_op jit(solution)/shard_map/all_gather | solution.py:148
  70.0 0.1 shard_map.67
  70.1 28.1 %all_to_all.17.parts_ref = bf16[16,16,512]{2,1,0:T(8,128)(2,1)S(1)} all-to-all(bf16[16,16,512]{2,1,0:T(8,128)(2,1)S(1)} %shard_map.67), channel_id=1, replica_groups=mesh['zh'=4,'y'=4,'core'=2,'x'=4,'zl'=4] {'zh','y'}, dimensions={0} | all-to-all | bytes 524288 | tf_op jit(solution)/shard_map/all_to_all | solution.py:149
  98.2 1.2 %shard_map.68 = bf16[1,16,512]{2,1,0:T(8,128)(2,1)} custom-call(s32[16]{0:T(128)S(1)} %copy-done, bf16[16,16,512]{2,1,0:T(8,128)(2,1)S(1)} %all_to_all.17.parts_ref), custom_call_target="tpu_custom_call" | custom-call | bytes 1048576 | tf_op jit(solution)/shard_map/pallas_call | solution.py:150
  (1 shorter events, 0.0 us)
Async XLA Ops:
  33.2 6.9 %collective-permute-start = (bf16[2,4,16,512]{3,2,1,0:T(8,128)(2,1)S(1)}, bf16[2,4,16,512]{3,2,1,0:T(8,128)(2,1)S(1)}, u32[]{:S(2)}, u32[]{:S(2)}) collective-permute-start(bf16[2,4,16,512]{3,2,1,0:T(8,128)(2,1)S(1)} %shard_map.64), channel_id=1, source_target_pairs={{0,4},{1,5},{4,8},{5,9},{6,2},{7,3},{8,12},{9,13},{10,6},{11,7},{1... | collective-permute-start | bytes 393224 | tf_op jit(solution)/shard_map/ppermute | solution.py:120
  40.1 23.9 %copy-start.2 = (bf16[4,1,512,512]{3,2,1,0:T(8,128)(2,1)S(1)}, bf16[4,1,512,512]{3,2,1,0:T(8,128)(2,1)}, u32[]{:S(2)}) copy-start(bf16[4,1,512,512]{3,2,1,0:T(8,128)(2,1)} %right_ref.1) | copy-start | bytes 6291460
  40.2 23.8 %copy-start = (s32[16]{0:T(128)S(1)}, s32[16]{0:T(128)}, u32[]{:S(2)}) copy-start(s32[16]{0:T(128)} %size_ref.3) | copy-start | bytes 196
  40.3 23.8 %copy-start.1 = (bf16[4,1,512,512]{3,2,1,0:T(8,128)(2,1)S(1)}, bf16[4,1,512,512]{3,2,1,0:T(8,128)(2,1)}, u32[]{:S(2)}) copy-start(bf16[4,1,512,512]{3,2,1,0:T(8,128)(2,1)} %left_ref.1) | copy-start | bytes 6291460
  40.3 23.8 %copy-start.3 = (s32[128]{0:T(128)S(1)}, s32[128]{0:T(128)}, u32[]{:S(2)}) copy-start(s32[128]{0:T(128)} %shift_ref.1) | copy-start | bytes 1540
  40.3 23.8 %copy-start.4 = (s32[4]{0:T(128)S(1)}, s32[4]{0:T(128)}, u32[]{:S(2)}) copy-start(s32[4]{0:T(128)} %assign_ref.1) | copy-start | bytes 52
  59.1 4.9 %collective-permute-start.1 = (bf16[4,5,4,16,512]{4,3,2,1,0:T(8,128)(2,1)S(1)}, bf16[4,5,4,16,512]{4,3,2,1,0:T(8,128)(2,1)S(1)}, u32[]{:S(2)}, u32[]{:S(2)}) collective-permute-start(bf16[4,5,4,16,512]{4,3,2,1,0:T(8,128)(2,1)S(1)} %all_to_all.16.mine_ref), channel_id=1, source_target_pairs={{0,16},{16,0},{1,17},{17,1},{2,18},{18,2},{3,19},{19,3},{4,20},{20... | collective-permute-start | bytes 3932168 | tf_op jit(solution)/shard_map/ppermute | solution.py:124

commit v3 on v2

--- a/solution.py
+++ b/solution.py
@@ -21,13 +21,6 @@
 
 def own_sector():
     return lax.axis_index("x") * ZL + lax.axis_index("zl")
-
-
-def live_mask(size, nblk):
-    term = (lax.axis_index("zh") * Y + lax.axis_index("y")) * CORE + lax.axis_index("core")
-    rows = term * SLAB + lax.broadcasted_iota(jnp.int32, (SLAB, nblk), 0)
-    cols = lax.broadcasted_iota(jnp.int32, (SLAB, nblk), 1)
-    return (rows < size) & (cols < size)
 
 
 def outgoing_kernel(column_ref, out_ref):
@@ -64,8 +57,9 @@
         for ref, of in ((mine_ref, core), (other_ref, 1 - core)):
             reach = jnp.maximum(inside + (y * CORE + of) * SLAB, cols)
             for place in range(NEAR):
-                live = jnp.where(reach < sizes[place], ref[y, place].astype(F32), 0.0)
-                blocks[place, :, y, pl.ds(of, 1)] = live.astype(BF16)[:, None]
+                block = ref[y, place]
+                live = jnp.where(reach < sizes[place], block, jnp.zeros_like(block))
+                blocks[place, :, y, pl.ds(of, 1)] = live[:, None]
     slots = left_ref.shape[0]
     for slot in range(slots):
         place = shift_ref[assign_ref[slot]] + 2
@@ -77,20 +71,23 @@
             total[...] = part
         else:
             total[...] += part
-    keep_ref[...] = total[:, core]
-    send_ref[...] = total[:, 1 - core].astype(BF16)
+    dims = keep_ref.shape
+    slab = lax.broadcasted_iota(jnp.int32, dims, 0) * (CORE * SLAB) + lax.broadcasted_iota(jnp.int32, dims, 1)
+    cols = lax.broadcasted_iota(jnp.int32, dims, 2)
+    for ref, of in ((keep_ref, core), (send_ref, 1 - core)):
+        reach = jnp.maximum(slab + of * SLAB, cols)
+        ref[...] = jnp.where(reach < sizes[2], total[:, of], 0.0).astype(ref.dtype)
 
 
 def join_kernel(keep_ref, both_ref, out_ref):
-    got = both_ref[1 - lax.axis_index("core")]
-    out_ref[...] = (keep_ref[...] + got.astype(F32)).astype(BF16)
+    core = lax.axis_index("core")
+    for place in range(ZH * Y):
+        joined = keep_ref[place] + both_ref[1 - core, place].astype(F32)
+        out_ref[jnp.where(core == 0, place, ZH * Y - 1 - place)] = joined.astype(BF16)
 
 
-def finish_kernel(size_ref, parts_ref, out_ref):
-    nblk = parts_ref.shape[-1]
-    total = jnp.sum(parts_ref[...].astype(F32), axis=0)
-    mask = live_mask(size_ref[own_sector()], nblk)
-    out_ref[0] = jnp.where(mask, total, 0.0).astype(BF16)
+def finish_kernel(parts_ref, out_ref):
+    out_ref[0] = jnp.sum(parts_ref[...].astype(F32), axis=0).astype(BF16)
 
 
 def call(kernel, out_shape, in_specs, scratch=(), flops=0, moved=MIB, limit=4 * MIB):
@@ -120,6 +117,12 @@
     return lax.ppermute(block, ("x", "zl"), route)
 
 
+def mirrored(block, axes):
+    members = range(0, block.shape[0] * CORE, CORE)
+    groups = [list(members), [member + 1 for member in reversed(members)]]
+    return lax.all_to_all(block, (*axes, "core"), 0, 0, tiled=True, axis_index_groups=groups)
+
+
 def swap_core(block):
     return lax.ppermute(block, "core", [(0, 1), (1, 0)])
 
@@ -146,8 +149,8 @@
         limit=12 * MIB,
     )(sector_size, charge_shift, assignment, mine, other, left_operator_blocks, right_ops)
     joined = call(join_kernel, shape(ZH * Y, SLAB, nblk), [VMEM, VMEM])(keep, lax.all_gather(send, "core"))
-    parts = lax.all_to_all(joined, ("zh", "y"), 0, 0, tiled=True)
-    return call(finish_kernel, shape(1, SLAB, nblk), [SMEM, VMEM])(sector_size, parts)
+    parts = mirrored(joined, ("zh", "y"))
+    return call(finish_kernel, shape(1, SLAB, nblk), [VMEM])(parts)
 
 
 def solution(mesh):

time: 101 us -> 98.9 us (0.979); the launches traced: 99.4 us -> 98.6 us
  no operation moved by 1% of the time
where the time goes in v3:
time: 98.9 us; the launch traced here: 98.6 us
  blocking collectives  81.6 us (83%)
  waiting for transfers between devices  8.56 us (9%)
  Pallas kernels  4.32 us (4%)
  starting transfers between devices  3.2 us (3%)
    all_to_all x1, blocking collectives, body(): lax.all_to_all(spread, ('zl', 'zh'), 0, 0, tiled=True)  32.5 us
    all_to_all x1, blocking collectives, mirrored(): lax.all_to_all(block, (*axes, 'core'), 0, 0, tiled=True, axis_index_group...  28.1 us
    all_to_all x1, blocking collectives, body(): mine = lax.all_to_all(near, 'y', 0, 0, tiled=True)  18.8 us
    ppermute x1, waiting for transfers between devices, next_x(): return lax.ppermute(block, ('x', 'zl'), route)  5.56 us
    pallas_call x1, Pallas kernels, body(): call(product_kernel, (shape(ZH * Y, SLAB, nblk, dtype=F32), shape(ZH * Y,...  3.48 us
    ppermute x1, waiting for transfers between devices, swap_core(): return lax.ppermute(block, 'core', [(0, 1), (1, 0)])  3 us
    all_gather x1, blocking collectives, body(): lax.all_gather(send, 'core')  2.18 us
  transfers between devices with their start and end apart: 2, of which 2 were waited for; matrix products, arithmetic and copies ran while one was open for 0% of the time, Pallas kernels for 0%

profile of v3, /device:TPU:6, one launch (start us, length us, event | category | flops | bytes accessed | tf_op | source)
XLA Modules:
  0.0 98.6 jit_solution(1824774883413065342)
XLA Ops:
  0.0 0.7 broadcast_in_dim.8
  0.7 32.5 %all_to_all.15 = bf16[16,16,512]{2,1,0:T(8,128)(2,1)S(1)} all-to-all(bf16[16,16,512]{2,1,0:T(8,128)(2,1)S(1)} %broadcast_in_dim.8), channel_id=1, replica_groups=mesh['zh'=4,'y'=4,'core'=2,'x'=4,'zl'=4] {'zl','zh'}, dimensions={0} | all-to-all | bytes 524288 | tf_op jit(solution)/shard_map/all_to_all | solution.py:134
  33.2 1.3 %collective-permute-start = (bf16[2,4,16,512]{3,2,1,0:T(8,128)(2,1)S(1)}, bf16[2,4,16,512]{3,2,1,0:T(8,128)(2,1)S(1)}, u32[]{:S(2)}, u32[]{:S(2)}) collective-permute-start(bf16[2,4,16,512]{3,2,1,0:T(8,128)(2,1)S(1)} %shard_map.64), channel_id=1, source_target_pairs={{0,4},{1,5},{4,8},{5,9},{6,2},{7,3},{8,12},{9,13},{10,6},{11,7},{1... | collective-permute-start | bytes 393224 | tf_op jit(solution)/shard_map/ppermute | solution.py:117
  34.5 5.6 %collective-permute-done.beside_ref = bf16[2,4,16,512]{3,2,1,0:T(8,128)(2,1)S(1)} collective-permute-done((bf16[2,4,16,512]{3,2,1,0:T(8,128)(2,1)S(1)}, bf16[2,4,16,512]{3,2,1,0:T(8,128)(2,1)S(1)}, u32[]{:S(2)}, u32[]{:S(2)}) %collective-permute-start) | collective-permute-done | bytes 131104 | tf_op jit(solution)/shard_map/ppermute | solution.py:117
  40.1 0.0 copy-start.1
  40.1 0.1 shard_map.65
  40.2 0.0 copy-start
  40.3 0.0 copy-start.2
  40.3 0.0 copy-start.3
  40.3 0.0 copy-start.4
  40.3 18.8 %all_to_all.16.mine_ref = bf16[4,5,4,16,512]{4,3,2,1,0:T(8,128)(2,1)S(1)} all-to-all(bf16[4,5,4,16,512]{4,3,2,1,0:T(8,128)(2,1)S(1)} %shard_map.65), channel_id=1, replica_groups=mesh['zh'=4,'y'=4,'core'=2,'x'=4,'zl'=4] {'y'}, dimensions={0} | all-to-all | bytes 2621440 | tf_op jit(solution)/shard_map/all_to_all | solution.py:137
  59.1 1.9 %collective-permute-start.1 = (bf16[4,5,4,16,512]{4,3,2,1,0:T(8,128)(2,1)S(1)}, bf16[4,5,4,16,512]{4,3,2,1,0:T(8,128)(2,1)S(1)}, u32[]{:S(2)}, u32[]{:S(2)}) collective-permute-start(bf16[4,5,4,16,512]{4,3,2,1,0:T(8,128)(2,1)S(1)} %all_to_all.16.mine_ref), channel_id=1, source_target_pairs={{0,16},{16,0},{1,17},{17,1},{2,18},{18,2},{3,19},{19,3},{4,20},{20... | collective-permute-start | bytes 3932168 | tf_op jit(solution)/shard_map/ppermute | solution.py:127
  61.1 3.0 %collective-permute-done.1.other_ref = bf16[4,5,4,16,512]{4,3,2,1,0:T(8,128)(2,1)S(1)} collective-permute-done((bf16[4,5,4,16,512]{4,3,2,1,0:T(8,128)(2,1)S(1)}, bf16[4,5,4,16,512]{4,3,2,1,0:T(8,128)(2,1)S(1)}, u32[]{:S(2)}, u32[]{:S(2)}) %collective-permute-start.1) | collective-permute-done | bytes 1310752 | tf_op jit(solution)/shard_map/ppermute | solution.py:127
  64.1 0.0 copy-done.1
  64.1 0.0 copy-done
  64.1 0.0 copy-done.2
  64.1 0.0 copy-done.3
  64.1 0.0 copy-done.4
  64.1 3.5 %shard_map.66 = (f32[16,16,512]{2,1,0:T(8,128)S(1)}, bf16[16,16,512]{2,1,0:T(8,128)(2,1)S(1)}) custom-call(s32[16]{0:T(128)S(1)} %copy-done.2, s32[128]{0:T(128)S(1)} %copy-done.3, s32[4]{0:T(128)S(1)} %copy-done.4, bf16[4,5,4,16,512]{4,3,2,1,0:T(8,128)(2,1)S(1)} %all_to_all.16.mine_ref, bf16[4,5,4,16,512]{4,3,2,1,0:T(8,128)(2,1)S(1)} %collective-permute-done.1.other_ref, ...), custom_call_target="tpu_custom_call" | custom-call | flops 2147483648 | bytes 8388608 | tf_op jit(solution)/shard_map/pallas_call | solution.py:139
  67.6 2.2 %all-gather = bf16[32,16,512]{2,1,0:T(8,128)(2,1)S(1)} all-gather(bf16[16,16,512]{2,1,0:T(8,128)(2,1)S(1)} %get-tuple-element.8), channel_id=2, replica_groups=mesh['zh'=4,'y'=4,'core'=2,'x'=4,'zl'=4] {'core'}, dimensions={0}, use_global_device_ids=true | all-gather | bytes 786432 | tf_op jit(solution)/shard_map/all_gather | solution.py:151
  69.8 0.1 shard_map.67
  69.8 28.1 %all_to_all.17.parts_ref = bf16[16,16,512]{2,1,0:T(8,128)(2,1)S(1)} all-to-all(bf16[16,16,512]{2,1,0:T(8,128)(2,1)S(1)} %shard_map.67), channel_id=1, replica_groups={{0,32,64,96,128,160,192,224,256,288,320,352,384,416,448,480},{496,464,4..., dimensions={0} | all-to-all | bytes 524288 | tf_op jit(solution)/shard_map/all_to_all | solution.py:123
  97.9 0.6 shard_map.68
  (1 shorter events, 0.0 us)
Async XLA Ops:
  33.2 6.9 %collective-permute-start = (bf16[2,4,16,512]{3,2,1,0:T(8,128)(2,1)S(1)}, bf16[2,4,16,512]{3,2,1,0:T(8,128)(2,1)S(1)}, u32[]{:S(2)}, u32[]{:S(2)}) collective-permute-start(bf16[2,4,16,512]{3,2,1,0:T(8,128)(2,1)S(1)} %shard_map.64), channel_id=1, source_target_pairs={{0,4},{1,5},{4,8},{5,9},{6,2},{7,3},{8,12},{9,13},{10,6},{11,7},{1... | collective-permute-start | bytes 393224 | tf_op jit(solution)/shard_map/ppermute | solution.py:117
  40.1 23.9 %copy-start.1 = (bf16[4,1,512,512]{3,2,1,0:T(8,128)(2,1)S(1)}, bf16[4,1,512,512]{3,2,1,0:T(8,128)(2,1)}, u32[]{:S(2)}) copy-start(bf16[4,1,512,512]{3,2,1,0:T(8,128)(2,1)} %right_ref.1) | copy-start | bytes 6291460
  40.2 23.8 %copy-start = (bf16[4,1,512,512]{3,2,1,0:T(8,128)(2,1)S(1)}, bf16[4,1,512,512]{3,2,1,0:T(8,128)(2,1)}, u32[]{:S(2)}) copy-start(bf16[4,1,512,512]{3,2,1,0:T(8,128)(2,1)} %left_ref.1) | copy-start | bytes 6291460
  40.3 23.8 %copy-start.2 = (s32[16]{0:T(128)S(1)}, s32[16]{0:T(128)}, u32[]{:S(2)}) copy-start(s32[16]{0:T(128)} %size_ref.1) | copy-start | bytes 196
  40.3 23.8 %copy-start.3 = (s32[128]{0:T(128)S(1)}, s32[128]{0:T(128)}, u32[]{:S(2)}) copy-start(s32[128]{0:T(128)} %shift_ref.1) | copy-start | bytes 1540
  40.3 23.8 %copy-start.4 = (s32[4]{0:T(128)S(1)}, s32[4]{0:T(128)}, u32[]{:S(2)}) copy-start(s32[4]{0:T(128)} %assign_ref.1) | copy-start | bytes 52
  59.1 4.9 %collective-permute-start.1 = (bf16[4,5,4,16,512]{4,3,2,1,0:T(8,128)(2,1)S(1)}, bf16[4,5,4,16,512]{4,3,2,1,0:T(8,128)(2,1)S(1)}, u32[]{:S(2)}, u32[]{:S(2)}) collective-permute-start(bf16[4,5,4,16,512]{4,3,2,1,0:T(8,128)(2,1)S(1)} %all_to_all.16.mine_ref), channel_id=1, source_target_pairs={{0,16},{16,0},{1,17},{17,1},{2,18},{18,2},{3,19},{19,3},{4,20},{20... | collective-permute-start | bytes 3932168 | tf_op jit(solution)/shard_map/ppermute | solution.py:127

commit v4 on v3

--- a/solution.py
+++ b/solution.py
@@ -11,6 +11,7 @@
 ZH, Y, CORE, X, ZL = 4, 4, 2, 4, 4
 SECTORS = X * ZL
 NEAR = 5
+GRAY = (0, 1, 3, 2)
 SLAB = 16
 F32, BF16 = jnp.float32, jnp.bfloat16
 
@@ -23,9 +24,18 @@
     return lax.axis_index("x") * ZL + lax.axis_index("zl")
 
 
+def gray(place):
+    return jnp.where(place < 2, place, 5 - place)
+
+
+def seat(core, place):
+    return jnp.where(core == 0, gray(place), 3 - gray(place))
+
+
 def outgoing_kernel(column_ref, out_ref):
     low = lax.axis_index("zl") < ZL // 2
-    out_ref[...] = column_ref[pl.ds(jnp.where(low, 2, 0), 2)]
+    for place in range(2):
+        out_ref[place] = column_ref[seat(lax.axis_index("core"), jnp.where(low, 2, 0) + place)]
 
 
 def pick_kernel(column_ref, beside_ref, out_ref):
@@ -35,7 +45,7 @@
 
         @pl.when((sector >= 0) & (sector < ZL))
         def _():
-            block = column_ref[jnp.clip(sector, 0, ZL - 1)]
+            block = column_ref[seat(lax.axis_index("core"), jnp.clip(sector, 0, ZL - 1))]
             for y in range(Y):
                 out_ref[y, place] = block
 
@@ -49,17 +59,18 @@
 def product_kernel(size_ref, shift_ref, assign_ref, mine_ref, other_ref, left_ref, right_ref, keep_ref, send_ref, blocks, total):
     core = lax.axis_index("core")
     nblk = left_ref.shape[-1]
-    dims = (ZH, SLAB, nblk)
-    inside = lax.broadcasted_iota(jnp.int32, dims, 0) * (Y * CORE * SLAB) + lax.broadcasted_iota(jnp.int32, dims, 1)
-    cols = lax.broadcasted_iota(jnp.int32, dims, 2)
+    row = lax.broadcasted_iota(jnp.int32, (SLAB, nblk), 0)
+    cols = lax.broadcasted_iota(jnp.int32, (SLAB, nblk), 1)
     sizes = [size_ref[jnp.clip(own_sector() + place - 2, 0, SECTORS - 1)] for place in range(NEAR)]
-    for y in range(Y):
-        for ref, of in ((mine_ref, core), (other_ref, 1 - core)):
-            reach = jnp.maximum(inside + (y * CORE + of) * SLAB, cols)
-            for place in range(NEAR):
-                block = ref[y, place]
-                live = jnp.where(reach < sizes[place], block, jnp.zeros_like(block))
-                blocks[place, :, y, pl.ds(of, 1)] = live[:, None]
+    for ref, of in ((mine_ref, core), (other_ref, 1 - core)):
+        for at in range(ZH):
+            zh = jnp.where(of == 0, GRAY[at], GRAY[3 - at])
+            for y in range(Y):
+                reach = jnp.maximum(((zh * Y + y) * CORE + of) * SLAB + row, cols)
+                for place in range(NEAR):
+                    block = ref[GRAY[y], place, at]
+                    live = jnp.where(reach < sizes[place], block, jnp.zeros_like(block))
+                    blocks[place, pl.ds(zh, 1), y, pl.ds(of, 1)] = live[None, None]
     slots = left_ref.shape[0]
     for slot in range(slots):
         place = shift_ref[assign_ref[slot]] + 2
@@ -81,9 +92,10 @@
 
 def join_kernel(keep_ref, both_ref, out_ref):
     core = lax.axis_index("core")
-    for place in range(ZH * Y):
-        joined = keep_ref[place] + both_ref[1 - core, place].astype(F32)
-        out_ref[jnp.where(core == 0, place, ZH * Y - 1 - place)] = joined.astype(BF16)
+    for zh in range(ZH):
+        for y in range(Y):
+            joined = keep_ref[zh * Y + y] + both_ref[1 - core, zh * Y + y].astype(F32)
+            out_ref[seat(core, y) * ZH + seat(core, zh)] = joined.astype(BF16)
 
 
 def finish_kernel(parts_ref, out_ref):
@@ -117,10 +129,15 @@
     return lax.ppermute(block, ("x", "zl"), route)
 
 
-def mirrored(block, axes):
-    members = range(0, block.shape[0] * CORE, CORE)
-    groups = [list(members), [member + 1 for member in reversed(members)]]
-    return lax.all_to_all(block, (*axes, "core"), 0, 0, tiled=True, axis_index_groups=groups)
+def exchange(block, outer, inner):
+    order = [(a * 4 + b) * CORE for a in GRAY for b in GRAY]
+    groups = [order, [member + 1 for member in reversed(order)]]
+    return lax.all_to_all(block, (outer, inner, "core"), 0, 0, tiled=True, axis_index_groups=groups)
+
+
+def exchange_y(block):
+    groups = [[y * CORE + core for y in GRAY] for core in range(CORE)]
+    return lax.all_to_all(block, ("y", "core"), 0, 0, tiled=True, axis_index_groups=groups)
 
 
 def swap_core(block):
@@ -131,10 +148,10 @@
     nblk = wavefunction.shape[2]
     slots = left_operator_blocks.shape[0]
     spread = jnp.broadcast_to(wavefunction, (ZL * ZH, SLAB, nblk))
-    column = lax.all_to_all(spread, ("zl", "zh"), 0, 0, tiled=True).reshape(ZL, ZH, SLAB, nblk)
+    column = exchange(spread, "zl", "zh").reshape(ZL, ZH, SLAB, nblk)
     beside = next_x(call(outgoing_kernel, shape(2, ZH, SLAB, nblk), [VMEM])(column))
     near = call(pick_kernel, shape(Y, NEAR, ZH, SLAB, nblk), [VMEM, VMEM])(column, beside)
-    mine = lax.all_to_all(near, "y", 0, 0, tiled=True)
+    mine = exchange_y(near)
     other = swap_core(mine)
     keep, send = call(
         product_kernel,
@@ -149,7 +166,7 @@
         limit=12 * MIB,
     )(sector_size, charge_shift, assignment, mine, other, left_operator_blocks, right_ops)
     joined = call(join_kernel, shape(ZH * Y, SLAB, nblk), [VMEM, VMEM])(keep, lax.all_gather(send, "core"))
-    parts = mirrored(joined, ("zh", "y"))
+    parts = exchange(joined, "y", "zh")
     return call(finish_kernel, shape(1, SLAB, nblk), [VMEM])(parts)
 
 

time: 98.9 us -> 95.5 us (0.966); the launches traced: 98.6 us -> 93.8 us
  blocking collectives: 81.6 us -> 76.9 us
    all_to_all x3, blocking collectives: 79.4 us -> 74.7 us  [the longest x2 58.2 us: exchange(): lax.all_to_all(block, (outer, inner, 'core'), 0, 0, tiled=True, axis_inde...]
where the time goes in v4:
time: 95.5 us; the launch traced here: 93.8 us
  blocking collectives  76.9 us (81%)
  waiting for transfers between devices  8.56 us (9%)
  Pallas kernels  4.28 us (4%)
  starting transfers between devices  3.2 us (3%)
    all_to_all x2, blocking collectives, exchange(): lax.all_to_all(block, (outer, inner, 'core'), 0, 0, tiled=True, axis_inde...  58.2 us
    all_to_all x1, blocking collectives, exchange_y(): lax.all_to_all(block, ('y', 'core'), 0, 0, tiled=True, axis_index_groups=...  16.5 us
    ppermute x1, waiting for transfers between devices, next_x(): return lax.ppermute(block, ('x', 'zl'), route)  5.56 us
    pallas_call x1, Pallas kernels, body(): call(product_kernel, (shape(ZH * Y, SLAB, nblk, dtype=F32), shape(ZH * Y,...  3.42 us
    ppermute x1, waiting for transfers between devices, swap_core(): return lax.ppermute(block, 'core', [(0, 1), (1, 0)])  3 us
    all_gather x1, blocking collectives, body(): lax.all_gather(send, 'core')  2.18 us
  transfers between devices with their start and end apart: 2, of which 2 were waited for; matrix products, arithmetic and copies ran while one was open for 0% of the time, Pallas kernels for 0%

profile of v4, /device:TPU:6, one launch (start us, length us, event | category | flops | bytes accessed | tf_op | source)
XLA Modules:
  0.0 93.8 jit_solution(8679677999320155439)
XLA Ops:
  0.0 0.7 broadcast_in_dim.8
  0.7 32.3 %all_to_all.15 = bf16[16,16,512]{2,1,0:T(8,128)(2,1)S(1)} all-to-all(bf16[16,16,512]{2,1,0:T(8,128)(2,1)S(1)} %broadcast_in_dim.8), channel_id=1, replica_groups={{0,128,384,256,1,129,385,257,3,131,387,259,2,130,386,258},{274,402,146,..., dimensions={0} | all-to-all | bytes 524288 | tf_op jit(solution)/shard_map/all_to_all | solution.py:135
  33.0 1.3 %collective-permute-start = (bf16[2,4,16,512]{3,2,1,0:T(8,128)(2,1)S(1)}, bf16[2,4,16,512]{3,2,1,0:T(8,128)(2,1)S(1)}, u32[]{:S(2)}, u32[]{:S(2)}) collective-permute-start(bf16[2,4,16,512]{3,2,1,0:T(8,128)(2,1)S(1)} %shard_map.64), channel_id=1, source_target_pairs={{0,4},{1,5},{4,8},{5,9},{6,2},{7,3},{8,12},{9,13},{10,6},{11,7},{1... | collective-permute-start | bytes 393224 | tf_op jit(solution)/shard_map/ppermute | solution.py:129
  34.3 5.6 %collective-permute-done.beside_ref = bf16[2,4,16,512]{3,2,1,0:T(8,128)(2,1)S(1)} collective-permute-done((bf16[2,4,16,512]{3,2,1,0:T(8,128)(2,1)S(1)}, bf16[2,4,16,512]{3,2,1,0:T(8,128)(2,1)S(1)}, u32[]{:S(2)}, u32[]{:S(2)}) %collective-permute-start) | collective-permute-done | bytes 131104 | tf_op jit(solution)/shard_map/ppermute | solution.py:129
  39.9 0.0 copy-start.1
  39.9 0.1 shard_map.65
  40.1 0.0 copy-start
  40.1 0.0 copy-start.2
  40.1 0.0 copy-start.3
  40.1 0.0 copy-start.4
  40.1 16.5 %all_to_all.16.mine_ref = bf16[4,5,4,16,512]{4,3,2,1,0:T(8,128)(2,1)S(1)} all-to-all(bf16[4,5,4,16,512]{4,3,2,1,0:T(8,128)(2,1)S(1)} %shard_map.65), channel_id=1, replica_groups={{0,32,96,64},{16,48,112,80},{1,33,97,65},{17,49,113,81},{2,34,98,66},{1..., dimensions={0} | all-to-all | bytes 2621440 | tf_op jit(solution)/shard_map/all_to_all | solution.py:140
  56.6 1.9 %collective-permute-start.1 = (bf16[4,5,4,16,512]{4,3,2,1,0:T(8,128)(2,1)S(1)}, bf16[4,5,4,16,512]{4,3,2,1,0:T(8,128)(2,1)S(1)}, u32[]{:S(2)}, u32[]{:S(2)}) collective-permute-start(bf16[4,5,4,16,512]{4,3,2,1,0:T(8,128)(2,1)S(1)} %all_to_all.16.mine_ref), channel_id=1, source_target_pairs={{0,16},{16,0},{1,17},{17,1},{2,18},{18,2},{3,19},{19,3},{4,20},{20... | collective-permute-start | bytes 3932168 | tf_op jit(solution)/shard_map/ppermute | solution.py:144
  58.6 3.0 %collective-permute-done.1.other_ref = bf16[4,5,4,16,512]{4,3,2,1,0:T(8,128)(2,1)S(1)} collective-permute-done((bf16[4,5,4,16,512]{4,3,2,1,0:T(8,128)(2,1)S(1)}, bf16[4,5,4,16,512]{4,3,2,1,0:T(8,128)(2,1)S(1)}, u32[]{:S(2)}, u32[]{:S(2)}) %collective-permute-start.1) | collective-permute-done | bytes 1310752 | tf_op jit(solution)/shard_map/ppermute | solution.py:144
  61.6 0.0 copy-done.1
  61.6 0.0 copy-done
  61.6 0.0 copy-done.2
  61.6 0.0 copy-done.3
  61.6 0.0 copy-done.4
  61.6 3.4 %shard_map.66 = (f32[16,16,512]{2,1,0:T(8,128)S(1)}, bf16[16,16,512]{2,1,0:T(8,128)(2,1)S(1)}) custom-call(s32[16]{0:T(128)S(1)} %copy-done.2, s32[128]{0:T(128)S(1)} %copy-done.3, s32[4]{0:T(128)S(1)} %copy-done.4, bf16[4,5,4,16,512]{4,3,2,1,0:T(8,128)(2,1)S(1)} %all_to_all.16.mine_ref, bf16[4,5,4,16,512]{4,3,2,1,0:T(8,128)(2,1)S(1)} %collective-permute-done.1.other_ref, ...), custom_call_target="tpu_custom_call" | custom-call | flops 2147483648 | bytes 8388608 | tf_op jit(solution)/shard_map/pallas_call | solution.py:156
  65.0 2.2 %all-gather = bf16[32,16,512]{2,1,0:T(8,128)(2,1)S(1)} all-gather(bf16[16,16,512]{2,1,0:T(8,128)(2,1)S(1)} %get-tuple-element.8), channel_id=2, replica_groups=mesh['zh'=4,'y'=4,'core'=2,'x'=4,'zl'=4] {'core'}, dimensions={0}, use_global_device_ids=true | all-gather | bytes 786432 | tf_op jit(solution)/shard_map/all_gather | solution.py:168
  67.2 0.1 shard_map.67
  67.3 25.9 %all_to_all.17.parts_ref = bf16[16,16,512]{2,1,0:T(8,128)(2,1)S(1)} all-to-all(bf16[16,16,512]{2,1,0:T(8,128)(2,1)S(1)} %shard_map.67), channel_id=1, replica_groups={{0,128,384,256,32,160,416,288,96,224,480,352,64,192,448,320},{336,464,2..., dimensions={0} | all-to-all | bytes 524288 | tf_op jit(solution)/shard_map/all_to_all | solution.py:135
  93.2 0.6 shard_map.68
  (1 shorter events, 0.0 us)
Async XLA Ops:
  33.0 6.9 %collective-permute-start = (bf16[2,4,16,512]{3,2,1,0:T(8,128)(2,1)S(1)}, bf16[2,4,16,512]{3,2,1,0:T(8,128)(2,1)S(1)}, u32[]{:S(2)}, u32[]{:S(2)}) collective-permute-start(bf16[2,4,16,512]{3,2,1,0:T(8,128)(2,1)S(1)} %shard_map.64), channel_id=1, source_target_pairs={{0,4},{1,5},{4,8},{5,9},{6,2},{7,3},{8,12},{9,13},{10,6},{11,7},{1... | collective-permute-start | bytes 393224 | tf_op jit(solution)/shard_map/ppermute | solution.py:129
  39.9 21.7 %copy-start.1 = (bf16[4,1,512,512]{3,2,1,0:T(8,128)(2,1)S(1)}, bf16[4,1,512,512]{3,2,1,0:T(8,128)(2,1)}, u32[]{:S(2)}) copy-start(bf16[4,1,512,512]{3,2,1,0:T(8,128)(2,1)} %right_ref.1) | copy-start | bytes 6291460
  40.1 21.5 %copy-start = (bf16[4,1,512,512]{3,2,1,0:T(8,128)(2,1)S(1)}, bf16[4,1,512,512]{3,2,1,0:T(8,128)(2,1)}, u32[]{:S(2)}) copy-start(bf16[4,1,512,512]{3,2,1,0:T(8,128)(2,1)} %left_ref.1) | copy-start | bytes 6291460
  40.1 21.5 %copy-start.2 = (s32[16]{0:T(128)S(1)}, s32[16]{0:T(128)}, u32[]{:S(2)}) copy-start(s32[16]{0:T(128)} %size_ref.1) | copy-start | bytes 196
  40.1 21.5 %copy-start.3 = (s32[128]{0:T(128)S(1)}, s32[128]{0:T(128)}, u32[]{:S(2)}) copy-start(s32[128]{0:T(128)} %shift_ref.1) | copy-start | bytes 1540
  40.1 21.5 %copy-start.4 = (s32[4]{0:T(128)S(1)}, s32[4]{0:T(128)}, u32[]{:S(2)}) copy-start(s32[4]{0:T(128)} %assign_ref.1) | copy-start | bytes 52
  56.6 4.9 %collective-permute-start.1 = (bf16[4,5,4,16,512]{4,3,2,1,0:T(8,128)(2,1)S(1)}, bf16[4,5,4,16,512]{4,3,2,1,0:T(8,128)(2,1)S(1)}, u32[]{:S(2)}, u32[]{:S(2)}) collective-permute-start(bf16[4,5,4,16,512]{4,3,2,1,0:T(8,128)(2,1)S(1)} %all_to_all.16.mine_ref), channel_id=1, source_target_pairs={{0,16},{16,0},{1,17},{17,1},{2,18},{18,2},{3,19},{19,3},{4,20},{20... | collective-permute-start | bytes 3932168 | tf_op jit(solution)/shard_map/ppermute | solution.py:144

commit v5 on v4

--- a/solution.py
+++ b/solution.py
@@ -95,7 +95,8 @@
     for zh in range(ZH):
         for y in range(Y):
             joined = keep_ref[zh * Y + y] + both_ref[1 - core, zh * Y + y].astype(F32)
-            out_ref[seat(core, y) * ZH + seat(core, zh)] = joined.astype(BF16)
+            place = jnp.where(core == 0, GRAY[y] * ZH + GRAY[zh], ZH * Y - 1 - (GRAY[zh] * Y + GRAY[y]))
+            out_ref[place] = joined.astype(BF16)
 
 
 def finish_kernel(parts_ref, out_ref):
@@ -129,9 +130,10 @@
     return lax.ppermute(block, ("x", "zl"), route)
 
 
-def exchange(block, outer, inner):
+def exchange(block, outer, inner, turned=False):
     order = [(a * 4 + b) * CORE for a in GRAY for b in GRAY]
-    groups = [order, [member + 1 for member in reversed(order)]]
+    other = [(a * 4 + b) * CORE for b in GRAY for a in GRAY] if turned else order
+    groups = [order, [member + 1 for member in reversed(other)]]
     return lax.all_to_all(block, (outer, inner, "core"), 0, 0, tiled=True, axis_index_groups=groups)
 
 
@@ -166,7 +168,7 @@
         limit=12 * MIB,
     )(sector_size, charge_shift, assignment, mine, other, left_operator_blocks, right_ops)
     joined = call(join_kernel, shape(ZH * Y, SLAB, nblk), [VMEM, VMEM])(keep, lax.all_gather(send, "core"))
-    parts = exchange(joined, "y", "zh")
+    parts = exchange(joined, "y", "zh", turned=True)
     return call(finish_kernel, shape(1, SLAB, nblk), [VMEM])(parts)
 
 

time: 95.5 us -> 95.1 us (level)
  no operation moved by 1% of the time
where the time goes in v5:
time: 95.1 us; the launch traced here: 93.9 us
  blocking collectives  77 us (81%)
  waiting for transfers between devices  8.56 us (9%)
  Pallas kernels  4.28 us (5%)
  starting transfers between devices  3.2 us (3%)
    all_to_all x2, blocking collectives, exchange(): lax.all_to_all(block, (outer, inner, 'core'), 0, 0, tiled=True, axis_inde...  58.2 us
    all_to_all x1, blocking collectives, exchange_y(): lax.all_to_all(block, ('y', 'core'), 0, 0, tiled=True, axis_index_groups=...  16.5 us
    ppermute x1, waiting for transfers between devices, next_x(): return lax.ppermute(block, ('x', 'zl'), route)  5.56 us
    pallas_call x1, Pallas kernels, body(): call(product_kernel, (shape(ZH * Y, SLAB, nblk, dtype=F32), shape(ZH * Y,...  3.42 us
    ppermute x1, waiting for transfers between devices, swap_core(): return lax.ppermute(block, 'core', [(0, 1), (1, 0)])  3 us
    all_gather x1, blocking collectives, body(): lax.all_gather(send, 'core')  2.18 us
    ppermute x1, starting transfers between devices, swap_core(): return lax.ppermute(block, 'core', [(0, 1), (1, 0)])  1.91 us
  transfers between devices with their start and end apart: 2, of which 2 were waited for; matrix products, arithmetic and copies ran while one was open for 0% of the time, Pallas kernels for 0%

profile of v5, /device:TPU:6, one launch (start us, length us, event | category | flops | bytes accessed | tf_op | source)
XLA Modules:
  0.0 93.9 jit_solution(18278458354792930090)
XLA Ops:
  0.0 0.7 broadcast_in_dim.8
  0.7 32.3 %all_to_all.15 = bf16[16,16,512]{2,1,0:T(8,128)(2,1)S(1)} all-to-all(bf16[16,16,512]{2,1,0:T(8,128)(2,1)S(1)} %broadcast_in_dim.8), channel_id=1, replica_groups={{0,128,384,256,1,129,385,257,3,131,387,259,2,130,386,258},{274,402,146,..., dimensions={0} | all-to-all | bytes 524288 | tf_op jit(solution)/shard_map/all_to_all | solution.py:137
  33.0 1.3 %collective-permute-start = (bf16[2,4,16,512]{3,2,1,0:T(8,128)(2,1)S(1)}, bf16[2,4,16,512]{3,2,1,0:T(8,128)(2,1)S(1)}, u32[]{:S(2)}, u32[]{:S(2)}) collective-permute-start(bf16[2,4,16,512]{3,2,1,0:T(8,128)(2,1)S(1)} %shard_map.64), channel_id=1, source_target_pairs={{0,4},{1,5},{4,8},{5,9},{6,2},{7,3},{8,12},{9,13},{10,6},{11,7},{1... | collective-permute-start | bytes 393224 | tf_op jit(solution)/shard_map/ppermute | solution.py:130
  34.3 5.6 %collective-permute-done.beside_ref = bf16[2,4,16,512]{3,2,1,0:T(8,128)(2,1)S(1)} collective-permute-done((bf16[2,4,16,512]{3,2,1,0:T(8,128)(2,1)S(1)}, bf16[2,4,16,512]{3,2,1,0:T(8,128)(2,1)S(1)}, u32[]{:S(2)}, u32[]{:S(2)}) %collective-permute-start) | collective-permute-done | bytes 131104 | tf_op jit(solution)/shard_map/ppermute | solution.py:130
  39.9 0.0 copy-start.1
  39.9 0.1 shard_map.65
  40.1 0.0 copy-start
  40.1 0.0 copy-start.2
  40.1 0.0 copy-start.3
  40.1 0.0 copy-start.4
  40.1 16.5 %all_to_all.16.mine_ref = bf16[4,5,4,16,512]{4,3,2,1,0:T(8,128)(2,1)S(1)} all-to-all(bf16[4,5,4,16,512]{4,3,2,1,0:T(8,128)(2,1)S(1)} %shard_map.65), channel_id=1, replica_groups={{0,32,96,64},{16,48,112,80},{1,33,97,65},{17,49,113,81},{2,34,98,66},{1..., dimensions={0} | all-to-all | bytes 2621440 | tf_op jit(solution)/shard_map/all_to_all | solution.py:142
  56.6 1.9 %collective-permute-start.1 = (bf16[4,5,4,16,512]{4,3,2,1,0:T(8,128)(2,1)S(1)}, bf16[4,5,4,16,512]{4,3,2,1,0:T(8,128)(2,1)S(1)}, u32[]{:S(2)}, u32[]{:S(2)}) collective-permute-start(bf16[4,5,4,16,512]{4,3,2,1,0:T(8,128)(2,1)S(1)} %all_to_all.16.mine_ref), channel_id=1, source_target_pairs={{0,16},{16,0},{1,17},{17,1},{2,18},{18,2},{3,19},{19,3},{4,20},{20... | collective-permute-start | bytes 3932168 | tf_op jit(solution)/shard_map/ppermute | solution.py:146
  58.6 3.0 %collective-permute-done.1.other_ref = bf16[4,5,4,16,512]{4,3,2,1,0:T(8,128)(2,1)S(1)} collective-permute-done((bf16[4,5,4,16,512]{4,3,2,1,0:T(8,128)(2,1)S(1)}, bf16[4,5,4,16,512]{4,3,2,1,0:T(8,128)(2,1)S(1)}, u32[]{:S(2)}, u32[]{:S(2)}) %collective-permute-start.1) | collective-permute-done | bytes 1310752 | tf_op jit(solution)/shard_map/ppermute | solution.py:146
  61.6 0.0 copy-done.1
  61.6 0.0 copy-done
  61.6 0.0 copy-done.2
  61.6 0.0 copy-done.3
  61.6 0.0 copy-done.4
  61.6 3.4 %shard_map.66 = (f32[16,16,512]{2,1,0:T(8,128)S(1)}, bf16[16,16,512]{2,1,0:T(8,128)(2,1)S(1)}) custom-call(s32[16]{0:T(128)S(1)} %copy-done.2, s32[128]{0:T(128)S(1)} %copy-done.3, s32[4]{0:T(128)S(1)} %copy-done.4, bf16[4,5,4,16,512]{4,3,2,1,0:T(8,128)(2,1)S(1)} %all_to_all.16.mine_ref, bf16[4,5,4,16,512]{4,3,2,1,0:T(8,128)(2,1)S(1)} %collective-permute-done.1.other_ref, ...), custom_call_target="tpu_custom_call" | custom-call | flops 2147483648 | bytes 8388608 | tf_op jit(solution)/shard_map/pallas_call | solution.py:158
  65.0 2.2 %all-gather = bf16[32,16,512]{2,1,0:T(8,128)(2,1)S(1)} all-gather(bf16[16,16,512]{2,1,0:T(8,128)(2,1)S(1)} %get-tuple-element.8), channel_id=2, replica_groups=mesh['zh'=4,'y'=4,'core'=2,'x'=4,'zl'=4] {'core'}, dimensions={0}, use_global_device_ids=true | all-gather | bytes 786432 | tf_op jit(solution)/shard_map/all_gather | solution.py:170
  67.2 0.1 shard_map.67
  67.3 26.0 %all_to_all.17.parts_ref = bf16[16,16,512]{2,1,0:T(8,128)(2,1)S(1)} all-to-all(bf16[16,16,512]{2,1,0:T(8,128)(2,1)S(1)} %shard_map.67), channel_id=1, replica_groups={{0,128,384,256,32,160,416,288,96,224,480,352,64,192,448,320},{336,368,3..., dimensions={0} | all-to-all | bytes 524288 | tf_op jit(solution)/shard_map/all_to_all | solution.py:137
  93.2 0.6 shard_map.68
  (1 shorter events, 0.0 us)
Async XLA Ops:
  33.0 6.9 %collective-permute-start = (bf16[2,4,16,512]{3,2,1,0:T(8,128)(2,1)S(1)}, bf16[2,4,16,512]{3,2,1,0:T(8,128)(2,1)S(1)}, u32[]{:S(2)}, u32[]{:S(2)}) collective-permute-start(bf16[2,4,16,512]{3,2,1,0:T(8,128)(2,1)S(1)} %shard_map.64), channel_id=1, source_target_pairs={{0,4},{1,5},{4,8},{5,9},{6,2},{7,3},{8,12},{9,13},{10,6},{11,7},{1... | collective-permute-start | bytes 393224 | tf_op jit(solution)/shard_map/ppermute | solution.py:130
  39.9 21.7 %copy-start.1 = (bf16[4,1,512,512]{3,2,1,0:T(8,128)(2,1)S(1)}, bf16[4,1,512,512]{3,2,1,0:T(8,128)(2,1)}, u32[]{:S(2)}) copy-start(bf16[4,1,512,512]{3,2,1,0:T(8,128)(2,1)} %right_ref.1) | copy-start | bytes 6291460
  40.1 21.5 %copy-start = (bf16[4,1,512,512]{3,2,1,0:T(8,128)(2,1)S(1)}, bf16[4,1,512,512]{3,2,1,0:T(8,128)(2,1)}, u32[]{:S(2)}) copy-start(bf16[4,1,512,512]{3,2,1,0:T(8,128)(2,1)} %left_ref.1) | copy-start | bytes 6291460
  40.1 21.5 %copy-start.2 = (s32[16]{0:T(128)S(1)}, s32[16]{0:T(128)}, u32[]{:S(2)}) copy-start(s32[16]{0:T(128)} %size_ref.1) | copy-start | bytes 196
  40.1 21.5 %copy-start.3 = (s32[128]{0:T(128)S(1)}, s32[128]{0:T(128)}, u32[]{:S(2)}) copy-start(s32[128]{0:T(128)} %shift_ref.1) | copy-start | bytes 1540
  40.1 21.5 %copy-start.4 = (s32[4]{0:T(128)S(1)}, s32[4]{0:T(128)}, u32[]{:S(2)}) copy-start(s32[4]{0:T(128)} %assign_ref.1) | copy-start | bytes 52
  56.6 4.9 %collective-permute-start.1 = (bf16[4,5,4,16,512]{4,3,2,1,0:T(8,128)(2,1)S(1)}, bf16[4,5,4,16,512]{4,3,2,1,0:T(8,128)(2,1)S(1)}, u32[]{:S(2)}, u32[]{:S(2)}) collective-permute-start(bf16[4,5,4,16,512]{4,3,2,1,0:T(8,128)(2,1)S(1)} %all_to_all.16.mine_ref), channel_id=1, source_target_pairs={{0,16},{16,0},{1,17},{17,1},{2,18},{18,2},{3,19},{19,3},{4,20},{20... | collective-permute-start | bytes 3932168 | tf_op jit(solution)/shard_map/ppermute | solution.py:146
